TPU v7x, 256 devices: a whole 4x4x8 slice. The times are simulated.
256 devices in a mesh: freq: 4 (over z_lo), shard: 64 (over x, z_hi, y, core).
Axes of the slice: x: 4, y: 4, z: 8 (z_hi: 2, z_lo: 4; z = z_hi * 4 + z_lo), core: 2. Of those that a mesh axis runs over, the one named last changes fastest.
Arguments:
- vis: float32 [4, 2, 2048, 1024], P('freq', None, 'shard'), may hold values from -6 to 6
- counts: int32 [1024], replicated, may hold values from 1 to 16
- band_start: int32 [1], replicated, may hold values from 0 to 1023
- beam: bfloat16 [4, 64, 2, 1024, 1024], P('freq', 'shard'), may hold values from -0.125 to 0.125
- legendre: bfloat16 [64, 1024, 1024], P('shard'), may hold values from -0.1875 to 0.1875
- cycle_index: int32 [1024], replicated, may hold values from 0 to 1023, each once
Outputs:
- sky_map: float32 [1024, 4096], P('shard')
Inputs may be any that keep to these rules, and one draw needn't show every extreme that they name: `cycle_index`: each latitude index appears once.
All inputs are finite; a program needn't handle non-finite values.
Results may differ from a plain program's by a relative error of at most 0.0041.
Values may be sent and summed in bfloat16 or wider, within the bound.
A program may use at most 64 MiB of HBM per device.

v0:
```python
import math

import jax
import jax.numpy as jnp
from jax import lax
from jax.sharding import PartitionSpec as P

NT = 2048
NPHI = 4096


def angle_table(first, count, steps, length):
    mvals = first + jnp.arange(count, dtype=jnp.int32)
    whole = mvals[:, None] * steps[None, :] % length
    return whole.astype(jnp.float32) * (2.0 * math.pi / length)


def local(vis, counts, band_start, beam, legendre, cycle_index):
    upper_limit = lax.Precision.HIGHEST
    shards = lax.axis_size("shard")
    mine = lax.axis_index("shard")
    first = band_start[0]
    local_modes = beam.shape[1]
    modes_total = local_modes * shards
    stream = vis[0]
    weight = counts.astype(jnp.float32) * (0.125 / math.sqrt(NT))
    block_list = lax.all_to_all(stream, "shard", split_axis=2, concat_axis=1, tiled=True)
    local_base = block_list.shape[2]
    time_angle = angle_table(first, modes_total, jnp.arange(NT, dtype=jnp.int32), NT)
    time_cosine = jnp.cos(time_angle)
    time_sine = jnp.sin(time_angle)
    visibility_real = block_list[0]
    visibility_imaginary = block_list[1]
    real_component = jnp.einsum(
        "wv,vg->wg", time_cosine, visibility_real, precision=upper_limit
    ) + jnp.einsum("wv,vg->wg", time_sine, visibility_imaginary, precision=upper_limit)
    imaginary_component = jnp.einsum(
        "wv,vg->wg", time_cosine, visibility_imaginary, precision=upper_limit
    ) - jnp.einsum("wv,vg->wg", time_sine, visibility_real, precision=upper_limit)
    local_weight = lax.dynamic_slice_in_dim(weight, mine * local_base, local_base)
    spectra = (jnp.stack([real_component, imaginary_component], axis=1) * local_weight).astype(
        jnp.bfloat16
    )
    visible = lax.all_to_all(spectra, "shard", split_axis=0, concat_axis=2, tiled=True)
    prod = jnp.einsum("mkla,mja->mkjl", beam[0], visible, preferred_element_type=jnp.float32)
    real_alm = prod[:, 0, 0] + prod[:, 1, 1]
    imag_alm = prod[:, 0, 1] - prod[:, 1, 0]
    harmonics = jnp.stack([real_alm, imag_alm], axis=1).astype(jnp.bfloat16)
    stored_order = jnp.einsum(
        "mkl,mlr->kmr", harmonics, legendre, preferred_element_type=jnp.float32
    )
    cycle_values = jnp.take(stored_order, cycle_index, axis=2)
    by_cycle = lax.all_to_all(cycle_values, "shard", split_axis=2, concat_axis=1, tiled=True)
    pixel_angle = angle_table(first, modes_total, jnp.arange(NPHI, dtype=jnp.int32), NPHI)
    pcos = jnp.cos(pixel_angle)
    psin = jnp.sin(pixel_angle)
    scale = 1.0 / math.sqrt(2.0 * modes_total)
    sky = (
        jnp.einsum("mr,mp->rp", by_cycle[0], pcos, precision=upper_limit)
        - jnp.einsum("mr,mp->rp", by_cycle[1], psin, precision=upper_limit)
    ) * scale
    sky = lax.psum(sky, "freq")
    return sky


def solution(mesh):
    return jax.shard_map(
        local,
        mesh=mesh,
        in_specs=(
            P("freq", None, "shard", None),
            P(),
            P(),
            P("freq", "shard", None, None, None),
            P("shard", None, None),
            P(),
        ),
        out_specs=P("shard", None),
        check_vma=False,
    )
```

profile of v0, /device:TPU:1, one launch (start us, length us, event | category | flops | bytes accessed | tf_op | source)
XLA Modules:
  0.0 173.3 jit_solution(1581387094253899854)
XLA Ops:
  6.5 2.3 %copy.13 = f32[1,2,32,1024]{2,1,3,0:T(2,128)} copy(f32[1,2,32,1024]{3,2,1,0:T(8,128)} %param.6) | data formatting | bytes 524288 | tf_op args[0]
  8.8 1.3 bitcast_bitcast_fusion
  10.1 1.8 %reshape.141 = f32[64,1,1024]{2,1,0:T(1,128)} reshape(f32[1024,2,32]{2,1,0:T(2,128)S(1)} %bitcast_bitcast_fusion) | data formatting | bytes 524288
  11.9 15.8 %all-to-all-start = ((f32[64,1,1024]{2,1,0:T(1,128)}), f32[64,1,1024]{2,1,0:T(1,128)S(1)}, u32[]{:S(2)}, u32[]{:S(2)}) async-start(f32[64,1,1024]{2,1,0:T(1,128)} %reshape.141), calls=%async_computation | async-start | bytes 524288 | tf_op jit(solution)/shard_map/all_to_all | solution.py:27
  28.3 0.1 dynamic_slice.3
  28.4 12.8 %all-to-all-done = f32[64,1,1024]{2,1,0:T(1,128)S(1)} async-done(((f32[64,1,1024]{2,1,0:T(1,128)}), f32[64,1,1024]{2,1,0:T(1,128)S(1)}, u32[]{:S(2)}, u32[]{:S(2)}) %all-to-all-start) | async-done | bytes 262176 | tf_op jit(solution)/shard_map/all_to_all | solution.py:27
  41.3 0.5 broadcast.67
  41.8 1.3 reduce.4
  43.0 0.9 reshape.142
  44.1 0.2 copy.16
  44.3 0.2 squeeze.26
  44.5 0.2 copy.15
  44.7 0.2 squeeze.25
  44.9 2.5 %fusion.29 = f32[64,16]{0,1:T(8,128)S(1)} fusion(f32[2048,16]{0,1:T(8,128)S(1)} %squeeze.26, s32[64]{0:T(128)S(1)} %iota_add_fusion), kind=kOutput, calls=%fused_computation.38 | convolution fusion | flops 27000832 | bytes 135424 | tf_op jit(solution)/shard_map/wv,vg->wg/dot_general | solution.py:37
  47.4 2.5 %fusion.31 = f32[64,16]{0,1:T(8,128)S(1)} fusion(f32[2048,16]{0,1:T(8,128)S(1)} %squeeze.25, s32[64]{0:T(128)S(1)} %iota_add_fusion), kind=kOutput, calls=%fused_computation.39 | convolution fusion | flops 27000832 | bytes 135424 | tf_op jit(solution)/shard_map/wv,vg->wg/dot_general | solution.py:34
  49.9 2.5 %fusion.8 = f32[64,1,16]{0,2,1:T(8,128)S(1)} fusion(f32[64,16]{0,1:T(8,128)S(1)} %fusion.29, f32[2048,16]{0,1:T(8,128)S(1)} %squeeze.25, s32[64]{0:T(128)S(1)} %iota_add_fusion), kind=kOutput, calls=%fused_computation.12 | convolution fusion | flops 27001856 | bytes 139520 | tf_op jit(solution)/shard_map/wv,vg->wg/dot_general | solution.py:39
  52.4 2.7 %fusion.9 = f32[64,1,16]{0,2,1:T(8,128)S(1)} fusion(f32[64,16]{0,1:T(8,128)S(1)} %fusion.31, f32[2048,16]{0,1:T(8,128)S(1)} %squeeze.26, s32[64]{0:T(128)S(1)} %iota_add_fusion), kind=kOutput, calls=%fused_computation.14 | convolution fusion | flops 27001856 | bytes 139520 | tf_op jit(solution)/shard_map/wv,vg->wg/dot_general | solution.py:36
  55.2 0.1 fusion.35
  55.3 0.7 copy.17
  56.0 4.6 %all-to-all-start.1 = ((bf16[64,2,16]{2,1,0:T(2,128)(2,1)}), bf16[64,2,16]{2,1,0:T(2,128)(2,1)S(1)}, u32[]{:S(2)}, u32[]{:S(2)}) async-start(bf16[64,2,16]{2,1,0:T(2,128)(2,1)} %copy.17), calls=%async_computation.1 | async-start | bytes 65536 | tf_op jit(solution)/shard_map/all_to_all | solution.py:44
  60.7 11.6 %all-to-all-done.1 = bf16[64,2,16]{2,1,0:T(2,128)(2,1)S(1)} async-done(((bf16[64,2,16]{2,1,0:T(2,128)(2,1)}), bf16[64,2,16]{2,1,0:T(2,128)(2,1)S(1)}, u32[]{:S(2)}, u32[]{:S(2)}) %all-to-all-start.1) | async-done | bytes 4128 | tf_op jit(solution)/shard_map/all_to_all | solution.py:44
  72.3 0.1 reshape.137
  72.4 3.4 %fusion.5 = f32[1,2,2,1024]{3,2,1,0:T(2,128)S(1)} fusion(bf16[2,1024,1]{1,0,2:T(2,128)(2,1)S(1)} %reshape.137, bf16[1,1,2,1024,1024]{4,3,2,1,0:T(8,128)(2,1)} %param.9), kind=kOutput, calls=%fused_computation.10 | convolution fusion | flops 8388608 | bytes 4214784 | tf_op jit(solution)/shard_map/mkla,mja->mkjl/dot_general | solution.py:45
  75.8 0.9 fusion.3
  76.7 2.8 %gather_fusion = f32[1024,2]{1,0:T(8,128)S(1)} fusion(f32[2,1024]{0,1:T(8,128)S(1)} %fusion.3, s32[1024]{0:T(1024)S(1)} %fusion.43), kind=kCustom, calls=%fused_computation | custom fusion | bytes 20480 | tf_op jit(solution)/shard_map/jit(_take)/gather | solution.py:52
  79.6 0.2 bitcast_select_fusion
  79.8 21.8 %all_to_all.39 = f32[2,1,1024]{0,1,2:T(1,128)S(1)} all-to-all(f32[2,1,1024]{0,1,2:T(1,128)S(1)} %bitcast.57), channel_id=1, replica_groups=mesh['freq'=4,'shard'=64] {'shard'}, dimensions={2} | all-to-all | bytes 16384 | tf_op jit(solution)/shard_map/all_to_all | solution.py:53
  101.5 6.2 %slice_reduce_fusion = (f32[1024]{0:T(1024)S(1)}, f32[1024]{0:T(1024)S(1)}) fusion(f32[2,1,1024]{0,1,2:T(1,128)S(1)} %all_to_all.39), kind=kLoop, calls=%fused_computation.30 | loop fusion | bytes 16384 | tf_op jit(solution)/shard_map/slice | solution.py:60
  107.8 4.5 %fusion.14 = f32[16,4096]{1,0:T(8,128)S(1)} fusion(f32[64,16]{1,0:T(8,128)S(1)} %squeeze.27, s32[64]{0:T(128)S(1)} %iota_add_fusion), kind=kOutput, calls=%fused_computation.19 | convolution fusion | flops 54001664 | bytes 266496 | tf_op jit(solution)/shard_map/mr,mp->rp/dot_general | solution.py:59
  112.4 5.5 %fusion = f32[16,4096]{1,0:T(8,128)} fusion(f32[16,4096]{1,0:T(8,128)S(1)} %fusion.14, f32[64,16]{1,0:T(8,128)S(1)} %squeeze.28, s32[64]{0:T(128)S(1)} %iota_add_fusion), kind=kOutput, calls=%fused_computation.2 | convolution fusion | flops 54132736 | bytes 528640 | tf_op jit(solution)/shard_map/mr,mp->rp/dot_general | solution.py:60
  117.9 46.9 %all-reduce.2.cloned.1.call-done = f32[16,4096]{1,0:T(8,128)} async-done(((f32[16,4096]{1,0:T(8,128)}), f32[16,4096]{1,0:T(8,128)}) %all-reduce.2.cloned.1.call-update) | async-done | bytes 262160 | tf_op jit(solution)/shard_map/psum | solution.py:62
  164.7 1.7 copy.24
  (18 shorter events, 0.4 us)
Async XLA Ops:
  6.5 69.3 %copy-start = (bf16[1,1024,1024]{2,1,0:T(8,128)(2,1)S(1)}, bf16[1,1024,1024]{2,1,0:T(8,128)(2,1)}, u32[]{:S(2)}) copy-start(bf16[1,1024,1024]{2,1,0:T(8,128)(2,1)} %param.10) | copy-start | bytes 6291460
  6.5 21.8 %copy-start.2 = (s32[1024]{0:T(1024)S(1)}, s32[1024]{0:T(1024)}, u32[]{:S(2)}) copy-start(s32[1024]{0:T(1024)} %param.7) | copy-start | bytes 12292
  6.5 21.9 %copy-start.1 = (s32[1024]{0:T(1024)S(1)}, s32[1024]{0:T(1024)}, u32[]{:S(2)}) copy-start(s32[1024]{0:T(1024)} %param.11) | copy-start | bytes 12292
  11.9 29.4 %all-to-all-start = ((f32[64,1,1024]{2,1,0:T(1,128)}), f32[64,1,1024]{2,1,0:T(1,128)S(1)}, u32[]{:S(2)}, u32[]{:S(2)}) async-start(f32[64,1,1024]{2,1,0:T(1,128)} %reshape.141), calls=%async_computation | async-start | bytes 524288 | tf_op jit(solution)/shard_map/all_to_all | solution.py:27
  56.0 16.3 %all-to-all-start.1 = ((bf16[64,2,16]{2,1,0:T(2,128)(2,1)}), bf16[64,2,16]{2,1,0:T(2,128)(2,1)S(1)}, u32[]{:S(2)}, u32[]{:S(2)}) async-start(bf16[64,2,16]{2,1,0:T(2,128)(2,1)} %copy.17), calls=%async_computation.1 | async-start | bytes 65536 | tf_op jit(solution)/shard_map/all_to_all | solution.py:44
  60.6 104.1 %all-reduce.2.cloned.1.call-start = ((), (), s32[]{:S(2)}) async-start(), calls=%async_computation.3 | async-start | bytes 524288 | tf_op jit(solution)/shard_map/psum | solution.py:62
Sparse Core Ops, SparseCore 0:
  118.0 46.7 all-reduce.1
where the time goes:
time: 175 us; the launch traced here: 173 us
  waiting for transfers between devices  71.3 us (41%)
  matrix products  24.5 us (14%)
  blocking collectives  21.8 us (12%)
  starting transfers between devices  20.4 us (12%)
  local copies, waits for them, and re-layouts  19.4 us (11%)
  between operations  14.2 us (8%)
    psum x1, waiting for transfers between devices, local(): sky = lax.psum(sky, 'freq')  46.9 us
    all_to_all x1, blocking collectives, local(): lax.all_to_all(cycle_values, 'shard', split_axis=2, concat_axis=1, tiled=...  21.8 us
    all_to_all x1, starting transfers between devices, local(): lax.all_to_all(stream, 'shard', split_axis=2, concat_axis=1, tiled=True)  15.8 us
    all_to_all x1, waiting for transfers between devices, local(): lax.all_to_all(stream, 'shard', split_axis=2, concat_axis=1, tiled=True)  12.8 us
    all_to_all x1, waiting for transfers between devices, local(): lax.all_to_all(spectra, 'shard', split_axis=0, concat_axis=2, tiled=True)  11.6 us
    unnamed x11, local copies, waits for them, and re-layouts  7.89 us
    slice x1, local copies, waits for them, and re-layouts, local(): by_cycle[1]  6.17 us
    dot_general x1, matrix products, local(): jnp.einsum('mr,mp->rp', by_cycle[1], psin, precision=upper_limit)  5.49 us
  transfers between devices with their start and end apart: 3, of which 3 were waited for; matrix products, arithmetic and copies ran while one was open for 0% of the time, Pallas kernels for 0%

commit v1 on v0

v1 whole, which is shorter than its diff:
```python
import functools
import math

import jax
import jax.numpy as jnp
from jax import lax
from jax.experimental import pallas as pl
from jax.experimental.pallas import tpu as pltpu
from jax.sharding import PartitionSpec as P

NT = 2048
NPHI = 4096
F32 = jnp.float32
BF16 = jnp.bfloat16
I32 = jnp.int32


def iota(shape, axis):
    return lax.broadcasted_iota(I32, shape, axis)


def cosine(turns, length):
    half = length // 2
    folded = ((turns + half) & (length - 1)) - half
    x = (length // 4 - jnp.abs(folded)).astype(F32) * (2.0 * math.pi / length)
    square = x * x
    total = jnp.full_like(x, 1.0 / math.factorial(13))
    for power, sign in ((11, -1), (9, 1), (7, -1), (5, 1), (3, -1), (1, 1)):
        total = total * square + sign / math.factorial(power)
    return total * x


def split(value):
    high = value.astype(BF16)
    return high, (value - high.astype(F32)).astype(BF16)


def mode_of(x, zh, y, c):
    return ((x * 2 + zh) * 4 + y) * 2 + c


def body(
    vis_hbm,
    counts_hbm,
    band_ref,
    beam_hbm,
    leg_hbm,
    index_hbm,
    out_ref,
    vis,
    counts,
    beam,
    leg,
    index,
    onehot,
    chosen,
    a_send,
    a_recv,
    b_send,
    b_recv,
    c_send,
    c_recv,
    d_send,
    d_recv,
    turned,
    load_sem,
    a_ssem,
    a_rsem,
    b_ssem,
    b_rsem,
    c_ssem,
    c_rsem,
    d_ssem,
    d_rsem,
):
    f = lax.axis_index("freq")
    s = lax.axis_index("shard")
    x, zh, y, c = s // 16, (s // 8) % 2, (s // 2) % 4, s % 2

    def shard_of(px, pz, py, pc):
        return ((px * 2 + pz) * 4 + py) * 2 + pc

    def plane(d):
        return f, shard_of((x + d // 4) % 4, zh, (y + d % 4) % 4, c)

    def column(df, e):
        return (f + df) % 4, shard_of(x, (zh + e // 2) % 2, y, (c + e % 2) % 2)

    barrier = pltpu.get_barrier_semaphore()
    partners = [plane(d) for d in range(1, 16)]
    partners += [column(q // 4, q % 4) for q in range(1, 16)]
    for partner in partners:
        pl.semaphore_signal(
            barrier, inc=1, device_id=partner, device_id_type=pl.DeviceIdType.MESH
        )

    def load(src, dst, i):
        copy = pltpu.make_async_copy(src, dst, load_sem.at[i])
        copy.start()
        return copy

    loads = [
        load(vis_hbm.at[0], vis, 0),
        load(index_hbm, index, 1),
        load(counts_hbm, counts, 2),
        load(leg_hbm.at[0], leg, 3),
        load(beam_hbm.at[0, 0], beam, 4),
    ]

    first = band_ref[0]

    row, col = iota((128, 256), 0), iota((128, 256), 1)
    d, e, ri = row >> 3, (row >> 1) & 3, row & 1
    k = mode_of((x + (d >> 2)) & 3, (zh + (e >> 1)) & 1, (y + (d & 3)) & 3, (c + e) & 1)
    ri_in = (col >> 5) & 1
    time = s * 32 + (col & 31)
    turns = (first + k) * time + (ri - ri_in) * (NT // 4)
    table_hi, table_lo = split(cosine(turns, NT))
    table = jnp.where(((col >> 6) & 1) == 1, table_lo.astype(F32), table_hi.astype(F32)).astype(BF16)
    loads[0].wait()
    vis_hi, vis_lo = split(vis[...].reshape(64, 1024))
    stream = jnp.concatenate([vis_hi, vis_hi, vis_lo, vis_lo], axis=0)
    a_send[...] = jnp.dot(table, stream, preferred_element_type=F32).reshape(16, 8, 1024)

    pl.semaphore_wait(barrier, 30)

    def send(src, dst, ssem, rsem, target):
        copy = pltpu.make_async_remote_copy(
            src_ref=src,
            dst_ref=dst,
            send_sem=ssem,
            recv_sem=rsem,
            device_id=target,
            device_id_type=pl.DeviceIdType.MESH,
        )
        copy.start()
        return copy

    a_copies = [
        send(a_send.at[d], a_recv.at[d], a_ssem.at[d], a_rsem.at[d], plane(d))
        for d in range(1, 16)
    ]

    loads[1].wait()
    stored = index[...]
    lane = iota((8, 128), 1)
    group = lane >> 4
    pieces = []
    for block in range(4):
        for half in range(2):
            joined = jnp.zeros((8, 128), I32)
            for part in range(8):
                px, py = half * 2 + part // 4, part % 4
                source = py * 2 + block % 2
                line = jnp.broadcast_to(stored[px * 2 + block // 2 : px * 2 + block // 2 + 1], (8, 128))
                shift = ((part - source) * 16) % 128
                if shift:
                    line = pltpu.roll(line, shift, 1)
                joined = jnp.where(group == part, line, joined)
            pieces.append(joined)
    for piece in range(8):
        wanted = jnp.broadcast_to(pieces[piece][0:1], (1024, 128))
        onehot[:, piece * 128 : piece * 128 + 128] = jnp.where(
            iota((1024, 128), 0) == wanted, 1.0, 0.0
        ).astype(BF16)
    loads[3].wait()
    for block in range(4):
        chosen[:, block * 256 : block * 256 + 256] = jnp.dot(
            leg[...], onehot[:, block * 256 : block * 256 + 256], preferred_element_type=F32
        ).astype(BF16)

    def sender_mode(r):
        d, e = r >> 3, (r >> 1) & 3
        return mode_of((x - (d >> 2)) & 3, (zh + (e >> 1)) & 1, (y - (d & 3)) & 3, (c + e) & 1)

    row, col = iota((128, 128), 0), iota((128, 128), 1)
    fine = cosine((first + sender_mode(row)) * col + (row & 1) * (NPHI // 4), NPHI)
    fine_hi, fine_lo = split(fine * (1.0 / math.sqrt(128.0)))
    row, col = iota((32, 128), 0), iota((32, 128), 1)
    turns = (first + sender_mode(col)) * row
    coarse_cos = cosine(turns, 32)
    coarse_sin = cosine(turns + 8 - 16 * (col & 1), 32)

    loads[2].wait()
    weight8 = counts[...].astype(F32) * (0.125 / math.sqrt(NT))
    weight = jnp.concatenate([weight8[i : i + 1] for i in range(8)], axis=1)

    total = a_send[0]
    for d in range(1, 16):
        a_copies[d - 1].wait_recv()
        total = total + a_recv[d]

    b_copies = []
    for e in range(1, 4):
        b_send[e] = total[2 * e : 2 * e + 2]
        b_copies.append(send(b_send.at[e], b_recv.at[e], b_ssem.at[e], b_rsem.at[e], column(0, e)))
    modes = total[0:2]
    for e in range(1, 4):
        b_copies[e - 1].wait_recv()
        modes = modes + b_recv[e]
    modes = modes * weight

    zeros = jnp.zeros((14, 1024), F32)
    direct = jnp.concatenate([modes, zeros], axis=0).astype(BF16)
    crossed = jnp.concatenate([modes[1:2], -modes[0:1], zeros], axis=0).astype(BF16)
    loads[4].wait()
    over_b = (((1,), (1,)), ((), ()))
    alm = lax.dot_general(direct, beam[0], over_b, preferred_element_type=F32)
    alm = alm + lax.dot_general(crossed, beam[1], over_b, preferred_element_type=F32)
    cycles = jnp.dot(alm.astype(BF16), chosen[...], preferred_element_type=F32)

    for block in range(4):
        c_send[block] = cycles[0:2, block * 256 : block * 256 + 256]
    c_copies = []
    for q in range(1, 16):
        e = q % 4
        block = ((zh + e // 2) % 2) * 2 + (c + e % 2) % 2
        c_copies.append(
            send(c_send.at[block], c_recv.at[q], c_ssem.at[q], c_rsem.at[q], column(q // 4, e))
        )
    mine = c_send[zh * 2 + c]
    sums = []
    for e in range(4):
        summed = mine
        for df in range(4):
            q = df * 4 + e
            if q:
                c_copies[q - 1].wait_recv()
            if df == 0:
                summed = c_recv[q] if q else mine
            else:
                summed = summed + c_recv[q]
        sums.append(summed)
    gathered = jnp.concatenate(sums, axis=0)
    d_send[0] = gathered[:, 0:128]
    d_send[1] = gathered[:, 128:256]

    d_copies = []
    for d in range(1, 16):
        half = ((x + d // 4) % 4) // 2
        d_copies.append(send(d_send.at[half], d_recv.at[d], d_ssem.at[d], d_rsem.at[d], plane(d)))
    d_recv[0] = d_send[x // 2]
    for copy in d_copies:
        copy.wait_recv()
    turned[...] = d_recv[...].reshape(128, 128).T
    place = (x % 2) * 4 + y
    values = turned[pl.ds(pl.multiple_of(place * 16, 16), 16), :]
    odd = (iota((16, 128), 1) & 1) == 1
    swapped = jnp.where(odd, pltpu.roll(values, 1, 1), pltpu.roll(values, 127, 1))
    moved = jnp.concatenate(
        [values * coarse_cos[a : a + 1] + swapped * coarse_sin[a : a + 1] for a in range(32)], axis=0
    )
    moved_hi, moved_lo = split(moved)
    image = jnp.dot(moved_hi, fine_hi, preferred_element_type=F32)
    image = image + jnp.dot(moved_lo, fine_hi, preferred_element_type=F32)
    image = image + jnp.dot(moved_hi, fine_lo, preferred_element_type=F32)
    for a in range(32):
        out_ref[:, a * 128 : a * 128 + 128] = image[a * 16 : a * 16 + 16]

    for copy in a_copies + b_copies + c_copies + d_copies:
        copy.wait_send()


def local(vis, counts, band_start, beam, legendre, cycle_index):
    anywhere = pl.BlockSpec(memory_space=pl.ANY)
    dma = pltpu.SemaphoreType.DMA
    return pl.pallas_call(
        body,
        out_shape=jax.ShapeDtypeStruct((16, NPHI), F32),
        in_specs=[
            anywhere,
            anywhere,
            pl.BlockSpec(memory_space=pltpu.SMEM),
            anywhere,
            anywhere,
            anywhere,
        ],
        out_specs=pl.BlockSpec(memory_space=pltpu.VMEM),
        scratch_shapes=[
            pltpu.VMEM((2, 32, 1024), F32),
            pltpu.VMEM((8, 128), I32),
            pltpu.VMEM((2, 1024, 1024), BF16),
            pltpu.VMEM((1024, 1024), BF16),
            pltpu.VMEM((8, 128), I32),
            pltpu.VMEM((1024, 1024), BF16),
            pltpu.VMEM((1024, 1024), BF16),
            pltpu.VMEM((16, 8, 1024), F32),
            pltpu.VMEM((16, 8, 1024), F32),
            pltpu.VMEM((4, 2, 1024), F32),
            pltpu.VMEM((4, 2, 1024), F32),
            pltpu.VMEM((4, 2, 256), F32),
            pltpu.VMEM((16, 2, 256), F32),
            pltpu.VMEM((2, 8, 128), F32),
            pltpu.VMEM((16, 8, 128), F32),
            pltpu.VMEM((128, 128), F32),
            dma((5,)),
            dma((16,)),
            dma((16,)),
            dma((4,)),
            dma((4,)),
            dma((16,)),
            dma((16,)),
            dma((16,)),
            dma((16,)),
        ],
        compiler_params=pltpu.CompilerParams(
            collective_id=0, has_side_effects=True, vmem_limit_bytes=56 * 1024 * 1024
        ),
    )(
        vis,
        counts.reshape(8, 128),
        band_start,
        beam,
        legendre,
        cycle_index.reshape(8, 128),
    )


def solution(mesh):
    return jax.shard_map(
        local,
        mesh=mesh,
        in_specs=(
            P("freq", None, "shard", None),
            P(),
            P(),
            P("freq", "shard", None, None, None),
            P("shard", None, None),
            P(),
        ),
        out_specs=P("shard", None),
        check_vma=False,
    )
```

time: 175 us -> 39.9 us (0.23)
  waiting for transfers between devices: 71.3 us -> 0 us
  Pallas kernels: 0 us -> 37.4 us
  matrix products: 24.5 us -> 0 us
  blocking collectives: 21.8 us -> 0 us
  starting transfers between devices: 20.4 us -> 0 us
  local copies, waits for them, and re-layouts: 19.4 us -> 1.67 us
  between operations: 14.2 us -> 0.66 us
    psum x1 -> x0, waiting for transfers between devices: 46.9 us -> none  [local(): sky = lax.psum(sky, 'freq')]
    pallas_call x0 -> x1, Pallas kernels: none -> 37.4 us  [local(): pl.pallas_call(body, out_shape=jax.ShapeDtypeStruct((16, NPHI), F32), in_...]
    dot_general x8 -> x0, matrix products: 24.5 us -> none  [the longest x1 5.49 us: local(): jnp.einsum('mr,mp->rp', by_cycle[1], psin, precision=upper_limit)]
    all_to_all x2 -> x0, waiting for transfers between devices: 24.4 us -> none  [the longest x1 12.8 us: local(): lax.all_to_all(stream, 'shard', split_axis=2, concat_axis=1, tiled=True)]
    all_to_all x1 -> x0, blocking collectives: 21.8 us -> none  [local(): lax.all_to_all(cycle_values, 'shard', split_axis=2, concat_axis=1, tiled=...]
    all_to_all x2 -> x0, starting transfers between devices: 20.4 us -> none  [the longest x1 15.8 us: local(): lax.all_to_all(stream, 'shard', split_axis=2, concat_axis=1, tiled=True)]
    slice x4 -> x0, local copies, waits for them, and re-layouts: 6.59 us -> none  [the longest x1 6.17 us: local(): by_cycle[1]]
    unnamed x11 -> x1, local copies, waits for them, and re-layouts: 7.89 us -> 1.67 us
  transfers between devices with their start and end apart: 3 -> 0, of which waited for: 3 -> 0; matrix products, arithmetic and copies ran while one was open for 0% -> 0% of each run, Pallas kernels for 0% -> 0%
where the time goes in v1:
time: 39.9 us; the launch traced here: 39.8 us
  Pallas kernels  37.4 us (94%)
  local copies, waits for them, and re-layouts  1.67 us (4%)
  between operations  0.66 us (2%)
    pallas_call x1, Pallas kernels, local(): pl.pallas_call(body, out_shape=jax.ShapeDtypeStruct((16, NPHI), F32), in_...  37.4 us
    unnamed x1, local copies, waits for them, and re-layouts  1.67 us

profile of v1, /device:TPU:1, one launch (start us, length us, event | category | flops | bytes accessed | tf_op | source)
XLA Modules:
  0.0 39.8 jit_solution(2548700977189549652)
XLA Ops:
  0.7 37.4 %shard_map.64 = f32[16,4096]{1,0:T(8,128)} custom-call(f32[1,2,32,1024]{3,2,1,0:T(8,128)} %vis_hbm.1, s32[8,128]{1,0:T(8,128)} %bitcast.2, s32[1]{0:T(128)S(6)} %copy.8.band_ref, bf16[1,1,2,1024,1024]{4,3,2,1,0:T(8,128)(2,1)} %beam_hbm.1, bf16[1,1024,1024]{2,1,0:T(8,128)(2,1)} %leg_hbm.1, s32[8,128]{1,0:T(8,128)} %bitcast.3), custom_call_target="tpu_custom_call" | custom-call | tf_op jit(solution)/shard_map/pallas_call | solution.py:267
  38.1 1.7 %copy.9 = f32[16,4096]{1,0:T(8,128)} copy(f32[16,4096]{1,0:T(8,128)} %shard_map.64) | data formatting | bytes 524288

commit v2 on v1

--- a/solution.py
+++ b/solution.py
@@ -35,6 +35,14 @@
     return high, (value - high.astype(F32)).astype(BF16)
 
 
+def hops(d):
+    return min(d // 4, 4 - d // 4) + min(d % 4, 4 - d % 4)
+
+
+FAR_FIRST = sorted(range(1, 16), key=hops, reverse=True)
+COLUMN = [q for q in range(1, 16) if q % 4 >= 2] + [q for q in range(1, 16) if q % 4 < 2]
+
+
 def mode_of(x, zh, y, c):
     return ((x * 2 + zh) * 4 + y) * 2 + c
 
@@ -42,13 +50,15 @@
 def body(
     vis_hbm,
     counts_hbm,
-    band_ref,
+    band_hbm,
     beam_hbm,
     leg_hbm,
     index_hbm,
     out_ref,
     vis,
+    swapped_vis,
     counts,
+    band,
     beam,
     leg,
     index,
@@ -64,6 +74,7 @@
     d_recv,
     turned,
     load_sem,
+    core_sem,
     a_ssem,
     a_rsem,
     b_ssem,
@@ -99,29 +110,38 @@
         copy.start()
         return copy
 
+    band_load = load(band_hbm, band, 6)
     loads = [
-        load(vis_hbm.at[0], vis, 0),
+        load(vis_hbm.at[0, :, :, 0:512], vis.at[0], 0),
+        load(vis_hbm.at[0, :, :, 512:1024], vis.at[1], 5),
         load(index_hbm, index, 1),
         load(counts_hbm, counts, 2),
         load(leg_hbm.at[0], leg, 3),
         load(beam_hbm.at[0, 0], beam, 4),
     ]
 
-    first = band_ref[0]
+    band_load.wait()
+    first = band[0]
 
     row, col = iota((128, 256), 0), iota((128, 256), 1)
     d, e, ri = row >> 3, (row >> 1) & 3, row & 1
     k = mode_of((x + (d >> 2)) & 3, (zh + (e >> 1)) & 1, (y + (d & 3)) & 3, (c + e) & 1)
-    ri_in = (col >> 5) & 1
-    time = s * 32 + (col & 31)
-    turns = (first + k) * time + (ri - ri_in) * (NT // 4)
-    table_hi, table_lo = split(cosine(turns, NT))
-    table = jnp.where(((col >> 6) & 1) == 1, table_lo.astype(F32), table_hi.astype(F32)).astype(BF16)
+    quarter = (ri - ((col >> 5) & 1)) * (NT // 4)
+    low_part = ((col >> 6) & 1) == 1
+
+    def time_table(core):
+        time = ((s // 2) * 2 + core) * 32 + (col & 31)
+        high, low = split(cosine((first + k) * time + quarter, NT))
+        return jnp.where(low_part, low.astype(F32), high.astype(F32)).astype(BF16)
+
+    def spectrum(table, samples):
+        high, low = split(samples.reshape(64, 512))
+        stream = jnp.concatenate([high, high, low, low], axis=0)
+        return jnp.dot(table, stream, preferred_element_type=F32)
+
+    own_table, other_table = time_table(c), time_table(1 - c)
     loads[0].wait()
-    vis_hi, vis_lo = split(vis[...].reshape(64, 1024))
-    stream = jnp.concatenate([vis_hi, vis_hi, vis_lo, vis_lo], axis=0)
-    a_send[...] = jnp.dot(table, stream, preferred_element_type=F32).reshape(16, 8, 1024)
-
+    loads[1].wait()
     pl.semaphore_wait(barrier, 30)
 
     def send(src, dst, ssem, rsem, target):
@@ -136,12 +156,18 @@
         copy.start()
         return copy
 
+    swap = send(vis.at[1 - c], swapped_vis, core_sem.at[0], core_sem.at[1], (f, s + 1 - 2 * c))
+    partial = spectrum(own_table, vis[c])
+    swap.wait_recv()
+    partial = partial + spectrum(other_table, swapped_vis[...])
+    a_send[...] = partial.reshape(16, 8, 512)
+
     a_copies = [
         send(a_send.at[d], a_recv.at[d], a_ssem.at[d], a_rsem.at[d], plane(d))
-        for d in range(1, 16)
+        for d in FAR_FIRST
     ]
 
-    loads[1].wait()
+    loads[2].wait()
     stored = index[...]
     lane = iota((8, 128), 1)
     group = lane >> 4
@@ -163,47 +189,38 @@
         onehot[:, piece * 128 : piece * 128 + 128] = jnp.where(
             iota((1024, 128), 0) == wanted, 1.0, 0.0
         ).astype(BF16)
-    loads[3].wait()
+    loads[4].wait()
     for block in range(4):
         chosen[:, block * 256 : block * 256 + 256] = jnp.dot(
             leg[...], onehot[:, block * 256 : block * 256 + 256], preferred_element_type=F32
         ).astype(BF16)
 
-    def sender_mode(r):
-        d, e = r >> 3, (r >> 1) & 3
-        return mode_of((x - (d >> 2)) & 3, (zh + (e >> 1)) & 1, (y - (d & 3)) & 3, (c + e) & 1)
-
-    row, col = iota((128, 128), 0), iota((128, 128), 1)
-    fine = cosine((first + sender_mode(row)) * col + (row & 1) * (NPHI // 4), NPHI)
-    fine_hi, fine_lo = split(fine * (1.0 / math.sqrt(128.0)))
-    row, col = iota((32, 128), 0), iota((32, 128), 1)
-    turns = (first + sender_mode(col)) * row
-    coarse_cos = cosine(turns, 32)
-    coarse_sin = cosine(turns + 8 - 16 * (col & 1), 32)
-
-    loads[2].wait()
+    loads[3].wait()
     weight8 = counts[...].astype(F32) * (0.125 / math.sqrt(NT))
     weight = jnp.concatenate([weight8[i : i + 1] for i in range(8)], axis=1)
 
     total = a_send[0]
-    for d in range(1, 16):
-        a_copies[d - 1].wait_recv()
+    for d, copy in reversed(list(zip(FAR_FIRST, a_copies))):
+        copy.wait_recv()
         total = total + a_recv[d]
 
     b_copies = []
-    for e in range(1, 4):
+    for e in (2, 3, 1):
         b_send[e] = total[2 * e : 2 * e + 2]
         b_copies.append(send(b_send.at[e], b_recv.at[e], b_ssem.at[e], b_rsem.at[e], column(0, e)))
-    modes = total[0:2]
-    for e in range(1, 4):
-        b_copies[e - 1].wait_recv()
-        modes = modes + b_recv[e]
+    for copy in b_copies:
+        copy.wait_recv()
+    near = total[0:2] + b_recv[2]
+    far = b_recv[1] + b_recv[3]
+    modes = jnp.concatenate(
+        [jnp.where(c == 0, near, far), jnp.where(c == 0, far, near)], axis=1
+    )
     modes = modes * weight
 
     zeros = jnp.zeros((14, 1024), F32)
     direct = jnp.concatenate([modes, zeros], axis=0).astype(BF16)
     crossed = jnp.concatenate([modes[1:2], -modes[0:1], zeros], axis=0).astype(BF16)
-    loads[4].wait()
+    loads[5].wait()
     over_b = (((1,), (1,)), ((), ()))
     alm = lax.dot_general(direct, beam[0], over_b, preferred_element_type=F32)
     alm = alm + lax.dot_general(crossed, beam[1], over_b, preferred_element_type=F32)
@@ -211,12 +228,12 @@
 
     for block in range(4):
         c_send[block] = cycles[0:2, block * 256 : block * 256 + 256]
-    c_copies = []
-    for q in range(1, 16):
+    c_copies = {}
+    for q in COLUMN:
         e = q % 4
         block = ((zh + e // 2) % 2) * 2 + (c + e % 2) % 2
-        c_copies.append(
-            send(c_send.at[block], c_recv.at[q], c_ssem.at[q], c_rsem.at[q], column(q // 4, e))
+        c_copies[q] = send(
+            c_send.at[block], c_recv.at[q], c_ssem.at[q], c_rsem.at[q], column(q // 4, e)
         )
     mine = c_send[zh * 2 + c]
     sums = []
@@ -225,7 +242,7 @@
         for df in range(4):
             q = df * 4 + e
             if q:
-                c_copies[q - 1].wait_recv()
+                c_copies[q].wait_recv()
             if df == 0:
                 summed = c_recv[q] if q else mine
             else:
@@ -236,7 +253,7 @@
     d_send[1] = gathered[:, 128:256]
 
     d_copies = []
-    for d in range(1, 16):
+    for d in FAR_FIRST:
         half = ((x + d // 4) % 4) // 2
         d_copies.append(send(d_send.at[half], d_recv.at[d], d_ssem.at[d], d_rsem.at[d], plane(d)))
     d_recv[0] = d_send[x // 2]
@@ -245,55 +262,97 @@
     turned[...] = d_recv[...].reshape(128, 128).T
     place = (x % 2) * 4 + y
     values = turned[pl.ds(pl.multiple_of(place * 16, 16), 16), :]
+    out_ref[...] = values
+    for copy in [swap] + a_copies + b_copies + list(c_copies.values()) + d_copies:
+        copy.wait_send()
+
+
+def paint(band_hbm, values_hbm, out_hbm, band, values_ref, pieces, sem):
+    band_load = pltpu.make_async_copy(band_hbm, band, sem.at[0])
+    band_load.start()
+    values_load = pltpu.make_async_copy(values_hbm, values_ref, sem.at[1])
+    values_load.start()
+    band_load.wait()
+    first = band[0]
+    s = lax.axis_index("shard")
+    x, zh, y, c = s // 16, (s // 8) % 2, (s // 2) % 4, s % 2
+
+    def sender_mode(r):
+        d, e = r >> 3, (r >> 1) & 3
+        return mode_of((x - (d >> 2)) & 3, (zh + (e >> 1)) & 1, (y - (d & 3)) & 3, (c + e) & 1)
+
+    row, col = iota((128, 128), 0), iota((128, 128), 1)
+    fine = cosine((first + sender_mode(row)) * col + (row & 1) * (NPHI // 4), NPHI)
+    fine_hi, fine_lo = split(fine * (1.0 / math.sqrt(128.0)))
+    row, col = iota((32, 128), 0), iota((32, 128), 1)
+    turns = (first + sender_mode(col)) * row
+    coarse_cos = cosine(turns, 32)
+    coarse_sin = cosine(turns + 8 - 16 * (col & 1), 32)
+
+    values_load.wait()
+    values = values_ref[...]
     odd = (iota((16, 128), 1) & 1) == 1
     swapped = jnp.where(odd, pltpu.roll(values, 1, 1), pltpu.roll(values, 127, 1))
-    moved = jnp.concatenate(
-        [values * coarse_cos[a : a + 1] + swapped * coarse_sin[a : a + 1] for a in range(32)], axis=0
-    )
-    moved_hi, moved_lo = split(moved)
-    image = jnp.dot(moved_hi, fine_hi, preferred_element_type=F32)
-    image = image + jnp.dot(moved_lo, fine_hi, preferred_element_type=F32)
-    image = image + jnp.dot(moved_hi, fine_lo, preferred_element_type=F32)
-    for a in range(32):
-        out_ref[:, a * 128 : a * 128 + 128] = image[a * 16 : a * 16 + 16]
-
-    for copy in a_copies + b_copies + c_copies + d_copies:
-        copy.wait_send()
+    copies = []
+    for piece in range(4):
+        moved = jnp.concatenate(
+            [
+                values * coarse_cos[a : a + 1] + swapped * coarse_sin[a : a + 1]
+                for a in range(piece * 8, piece * 8 + 8)
+            ],
+            axis=0,
+        )
+        moved_hi, moved_lo = split(moved)
+        image = jnp.dot(moved_hi, fine_hi, preferred_element_type=F32)
+        image = image + jnp.dot(moved_lo, fine_hi, preferred_element_type=F32)
+        image = image + jnp.dot(moved_hi, fine_lo, preferred_element_type=F32)
+        for a in range(8):
+            pieces[piece, :, a * 128 : a * 128 + 128] = image[a * 16 : a * 16 + 16]
+        copy = pltpu.make_async_copy(
+            pieces.at[piece], out_hbm.at[:, piece * 1024 : piece * 1024 + 1024], sem.at[2 + piece]
+        )
+        copy.start()
+        copies.append(copy)
+    for copy in copies:
+        copy.wait()
 
 
 def local(vis, counts, band_start, beam, legendre, cycle_index):
     anywhere = pl.BlockSpec(memory_space=pl.ANY)
     dma = pltpu.SemaphoreType.DMA
-    return pl.pallas_call(
+    values = pl.pallas_call(
         body,
-        out_shape=jax.ShapeDtypeStruct((16, NPHI), F32),
+        out_shape=jax.ShapeDtypeStruct((16, 128), F32),
         in_specs=[
             anywhere,
             anywhere,
-            pl.BlockSpec(memory_space=pltpu.SMEM),
+            anywhere,
             anywhere,
             anywhere,
             anywhere,
         ],
         out_specs=pl.BlockSpec(memory_space=pltpu.VMEM),
         scratch_shapes=[
-            pltpu.VMEM((2, 32, 1024), F32),
+            pltpu.VMEM((2, 2, 32, 512), F32),
+            pltpu.VMEM((2, 32, 512), F32),
             pltpu.VMEM((8, 128), I32),
+            pltpu.SMEM((1,), I32),
             pltpu.VMEM((2, 1024, 1024), BF16),
             pltpu.VMEM((1024, 1024), BF16),
             pltpu.VMEM((8, 128), I32),
             pltpu.VMEM((1024, 1024), BF16),
             pltpu.VMEM((1024, 1024), BF16),
-            pltpu.VMEM((16, 8, 1024), F32),
-            pltpu.VMEM((16, 8, 1024), F32),
-            pltpu.VMEM((4, 2, 1024), F32),
-            pltpu.VMEM((4, 2, 1024), F32),
+            pltpu.VMEM((16, 8, 512), F32),
+            pltpu.VMEM((16, 8, 512), F32),
+            pltpu.VMEM((4, 2, 512), F32),
+            pltpu.VMEM((4, 2, 512), F32),
             pltpu.VMEM((4, 2, 256), F32),
             pltpu.VMEM((16, 2, 256), F32),
             pltpu.VMEM((2, 8, 128), F32),
             pltpu.VMEM((16, 8, 128), F32),
             pltpu.VMEM((128, 128), F32),
-            dma((5,)),
+            dma((7,)),
+            dma((2,)),
             dma((16,)),
             dma((16,)),
             dma((4,)),
@@ -314,6 +373,18 @@
         legendre,
         cycle_index.reshape(8, 128),
     )
+    return pl.pallas_call(
+        paint,
+        out_shape=jax.ShapeDtypeStruct((16, NPHI), F32),
+        in_specs=[anywhere, anywhere],
+        out_specs=anywhere,
+        scratch_shapes=[
+            pltpu.SMEM((1,), I32),
+            pltpu.VMEM((16, 128), F32),
+            pltpu.VMEM((4, 16, 1024), F32),
+            dma((6,)),
+        ],
+    )(band_start, values)
 
 
 def solution(mesh):

time: 39.9 us -> 37 us (0.927)
  local copies, waits for them, and re-layouts: 1.67 us -> 0 us
  Pallas kernels: 37.4 us -> 36.2 us
    unnamed x1 -> x0, local copies, waits for them, and re-layouts: 1.67 us -> none
    pallas_call x1 -> x2, Pallas kernels: 37.4 us -> 36.2 us  [the longest x1 34.4 us: local(): pl.pallas_call(body, out_shape=jax.ShapeDtypeStruct((16, 128), F32), in_s...]
where the time goes in v2:
time: 37 us; the launch traced here: 36.8 us
  Pallas kernels  36.2 us (98%)
  between operations  0.66 us (2%)
    pallas_call x1, Pallas kernels, local(): pl.pallas_call(body, out_shape=jax.ShapeDtypeStruct((16, 128), F32), in_s...  34.4 us
    pallas_call x1, Pallas kernels, local(): pl.pallas_call(paint, out_shape=jax.ShapeDtypeStruct((16, NPHI), F32), in...  1.72 us

profile of v2, /device:TPU:1, one launch (start us, length us, event | category | flops | bytes accessed | tf_op | source)
XLA Modules:
  0.0 36.8 jit_solution(14037015404784900970)
XLA Ops:
  0.7 34.4 %shard_map.64.values_hbm = f32[16,128]{1,0:T(8,128)} custom-call(f32[1,2,32,1024]{3,2,1,0:T(8,128)} %vis_hbm.1, s32[8,128]{1,0:T(8,128)} %bitcast.2, s32[1]{0:T(128)S(6)} %copy.7.band_hbm, bf16[1,1,2,1024,1024]{4,3,2,1,0:T(8,128)(2,1)} %beam_hbm.1, bf16[1,1024,1024]{2,1,0:T(8,128)(2,1)} %leg_hbm.1, s32[8,128]{1,0:T(8,128)} %bitcast.3), custom_call_target="tpu_custom_call" | custom-call | tf_op jit(solution)/shard_map/pallas_call | solution.py:323
  35.1 1.7 %shard_map.65 = f32[16,4096]{1,0:T(8,128)} custom-call(s32[1]{0:T(128)S(6)} %copy.7.band_hbm, f32[16,128]{1,0:T(8,128)} %shard_map.64.values_hbm), custom_call_target="tpu_custom_call" | custom-call | tf_op jit(solution)/shard_map/pallas_call | solution.py:376

commit v3 on v1

--- a/solution.py
+++ b/solution.py
@@ -35,6 +35,14 @@
     return high, (value - high.astype(F32)).astype(BF16)
 
 
+def hops(d):
+    return min(d // 4, 4 - d // 4) + min(d % 4, 4 - d % 4)
+
+
+FAR_FIRST = sorted(range(1, 16), key=hops, reverse=True)
+COLUMN = [q for q in range(1, 16) if q % 4 >= 2] + [q for q in range(1, 16) if q % 4 < 2]
+
+
 def mode_of(x, zh, y, c):
     return ((x * 2 + zh) * 4 + y) * 2 + c
 
@@ -42,13 +50,14 @@
 def body(
     vis_hbm,
     counts_hbm,
-    band_ref,
+    band_hbm,
     beam_hbm,
     leg_hbm,
     index_hbm,
     out_ref,
     vis,
     counts,
+    band,
     beam,
     leg,
     index,
@@ -56,6 +65,8 @@
     chosen,
     a_send,
     a_recv,
+    step_send,
+    step_recv,
     b_send,
     b_recv,
     c_send,
@@ -66,6 +77,8 @@
     load_sem,
     a_ssem,
     a_rsem,
+    step_ssem,
+    step_rsem,
     b_ssem,
     b_rsem,
     c_ssem,
@@ -87,8 +100,7 @@
         return (f + df) % 4, shard_of(x, (zh + e // 2) % 2, y, (c + e % 2) % 2)
 
     barrier = pltpu.get_barrier_semaphore()
-    partners = [plane(d) for d in range(1, 16)]
-    partners += [column(q // 4, q % 4) for q in range(1, 16)]
+    partners = [plane(d) for d in FAR_FIRST] + [column(q // 4, q % 4) for q in COLUMN]
     for partner in partners:
         pl.semaphore_signal(
             barrier, inc=1, device_id=partner, device_id_type=pl.DeviceIdType.MESH
@@ -99,6 +111,7 @@
         copy.start()
         return copy
 
+    band_load = load(band_hbm, band, 6)
     loads = [
         load(vis_hbm.at[0], vis, 0),
         load(index_hbm, index, 1),
@@ -107,20 +120,27 @@
         load(beam_hbm.at[0, 0], beam, 4),
     ]
 
-    first = band_ref[0]
+    band_load.wait()
+    first = band[0]
 
     row, col = iota((128, 256), 0), iota((128, 256), 1)
     d, e, ri = row >> 3, (row >> 1) & 3, row & 1
     k = mode_of((x + (d >> 2)) & 3, (zh + (e >> 1)) & 1, (y + (d & 3)) & 3, (c + e) & 1)
-    ri_in = (col >> 5) & 1
-    time = s * 32 + (col & 31)
-    turns = (first + k) * time + (ri - ri_in) * (NT // 4)
-    table_hi, table_lo = split(cosine(turns, NT))
-    table = jnp.where(((col >> 6) & 1) == 1, table_lo.astype(F32), table_hi.astype(F32)).astype(BF16)
+    quarter = (ri - ((col >> 5) & 1)) * (NT // 4)
+    table_hi, table_lo = split(cosine((first + k) * (s * 32 + (col & 31)) + quarter, NT))
+    low_part = ((col >> 6) & 1) == 1
+    table = jnp.where(low_part, table_lo.astype(F32), table_hi.astype(F32)).astype(BF16)
     loads[0].wait()
     vis_hi, vis_lo = split(vis[...].reshape(64, 1024))
     stream = jnp.concatenate([vis_hi, vis_hi, vis_lo, vis_lo], axis=0)
-    a_send[...] = jnp.dot(table, stream, preferred_element_type=F32).reshape(16, 8, 1024)
+    partial = jnp.dot(table, stream, preferred_element_type=F32)
+
+    for d in range(1, 16):
+        part = partial[d * 8 : d * 8 + 8]
+        part = jnp.concatenate([part[:, 0:512], part[:, 512:1024]], axis=0)
+        largest = jnp.maximum(jnp.max(jnp.abs(part), axis=(0, 1), keepdims=True), 1e-30)
+        a_send[d] = jnp.round(part * (32767.0 / largest)).astype(I32).astype(jnp.int16)
+        step_send[d] = jnp.broadcast_to(largest * (1.0 / 32767.0), (1, 128))
 
     pl.semaphore_wait(barrier, 30)
 
@@ -136,9 +156,13 @@
         copy.start()
         return copy
 
+    step_copies = [
+        send(step_send.at[d], step_recv.at[d], step_ssem.at[d], step_rsem.at[d], plane(d))
+        for d in FAR_FIRST
+    ]
     a_copies = [
         send(a_send.at[d], a_recv.at[d], a_ssem.at[d], a_rsem.at[d], plane(d))
-        for d in range(1, 16)
+        for d in FAR_FIRST
     ]
 
     loads[1].wait()
@@ -185,19 +209,21 @@
     weight8 = counts[...].astype(F32) * (0.125 / math.sqrt(NT))
     weight = jnp.concatenate([weight8[i : i + 1] for i in range(8)], axis=1)
 
-    total = a_send[0]
-    for d in range(1, 16):
-        a_copies[d - 1].wait_recv()
-        total = total + a_recv[d]
+    total = jnp.concatenate([partial[0:8, 0:512], partial[0:8, 512:1024]], axis=0)
+    for d, step_copy, copy in reversed(list(zip(FAR_FIRST, step_copies, a_copies))):
+        step_copy.wait_recv()
+        copy.wait_recv()
+        step = jnp.concatenate([step_recv[d]] * 4, axis=1)
+        total = total + a_recv[d].astype(I32).astype(F32) * step
+    total = jnp.concatenate([total[0:8], total[8:16]], axis=1)
 
     b_copies = []
-    for e in range(1, 4):
+    for e in (2, 3, 1):
         b_send[e] = total[2 * e : 2 * e + 2]
         b_copies.append(send(b_send.at[e], b_recv.at[e], b_ssem.at[e], b_rsem.at[e], column(0, e)))
-    modes = total[0:2]
-    for e in range(1, 4):
-        b_copies[e - 1].wait_recv()
-        modes = modes + b_recv[e]
+    for copy in b_copies:
+        copy.wait_recv()
+    modes = total[0:2] + b_recv[1] + b_recv[2] + b_recv[3]
     modes = modes * weight
 
     zeros = jnp.zeros((14, 1024), F32)
@@ -211,12 +237,12 @@
 
     for block in range(4):
         c_send[block] = cycles[0:2, block * 256 : block * 256 + 256]
-    c_copies = []
-    for q in range(1, 16):
+    c_copies = {}
+    for q in COLUMN:
         e = q % 4
         block = ((zh + e // 2) % 2) * 2 + (c + e % 2) % 2
-        c_copies.append(
-            send(c_send.at[block], c_recv.at[q], c_ssem.at[q], c_rsem.at[q], column(q // 4, e))
+        c_copies[q] = send(
+            c_send.at[block], c_recv.at[q], c_ssem.at[q], c_rsem.at[q], column(q // 4, e)
         )
     mine = c_send[zh * 2 + c]
     sums = []
@@ -225,7 +251,7 @@
         for df in range(4):
             q = df * 4 + e
             if q:
-                c_copies[q - 1].wait_recv()
+                c_copies[q].wait_recv()
             if df == 0:
                 summed = c_recv[q] if q else mine
             else:
@@ -236,7 +262,7 @@
     d_send[1] = gathered[:, 128:256]
 
     d_copies = []
-    for d in range(1, 16):
+    for d in FAR_FIRST:
         half = ((x + d // 4) % 4) // 2
         d_copies.append(send(d_send.at[half], d_recv.at[d], d_ssem.at[d], d_rsem.at[d], plane(d)))
     d_recv[0] = d_send[x // 2]
@@ -257,7 +283,7 @@
     for a in range(32):
         out_ref[:, a * 128 : a * 128 + 128] = image[a * 16 : a * 16 + 16]
 
-    for copy in a_copies + b_copies + c_copies + d_copies:
+    for copy in step_copies + a_copies + b_copies + list(c_copies.values()) + d_copies:
         copy.wait_send()
 
 
@@ -266,11 +292,11 @@
     dma = pltpu.SemaphoreType.DMA
     return pl.pallas_call(
         body,
-        out_shape=jax.ShapeDtypeStruct((16, NPHI), F32),
+        out_shape=pltpu.VMEM((16, NPHI), F32),
         in_specs=[
             anywhere,
             anywhere,
-            pl.BlockSpec(memory_space=pltpu.SMEM),
+            anywhere,
             anywhere,
             anywhere,
             anywhere,
@@ -279,13 +305,16 @@
         scratch_shapes=[
             pltpu.VMEM((2, 32, 1024), F32),
             pltpu.VMEM((8, 128), I32),
+            pltpu.SMEM((1,), I32),
             pltpu.VMEM((2, 1024, 1024), BF16),
             pltpu.VMEM((1024, 1024), BF16),
             pltpu.VMEM((8, 128), I32),
             pltpu.VMEM((1024, 1024), BF16),
             pltpu.VMEM((1024, 1024), BF16),
-            pltpu.VMEM((16, 8, 1024), F32),
-            pltpu.VMEM((16, 8, 1024), F32),
+            pltpu.VMEM((16, 16, 512), jnp.int16),
+            pltpu.VMEM((16, 16, 512), jnp.int16),
+            pltpu.VMEM((16, 1, 128), F32),
+            pltpu.VMEM((16, 1, 128), F32),
             pltpu.VMEM((4, 2, 1024), F32),
             pltpu.VMEM((4, 2, 1024), F32),
             pltpu.VMEM((4, 2, 256), F32),
@@ -293,7 +322,9 @@
             pltpu.VMEM((2, 8, 128), F32),
             pltpu.VMEM((16, 8, 128), F32),
             pltpu.VMEM((128, 128), F32),
-            dma((5,)),
+            dma((7,)),
+            dma((16,)),
+            dma((16,)),
             dma((16,)),
             dma((16,)),
             dma((4,)),
@@ -314,7 +345,6 @@
         legendre,
         cycle_index.reshape(8, 128),
     )
-
 
 def solution(mesh):
     return jax.shard_map(

time: 39.9 us -> 34.8 us (0.87)
  Pallas kernels: 37.4 us -> 33.3 us
  local copies, waits for them, and re-layouts: 1.67 us -> 0.71 us
    pallas_call x1, Pallas kernels: 37.4 us -> 33.3 us  [local(): pl.pallas_call(body, out_shape=pltpu.VMEM((16, NPHI), F32), in_specs=[any...]
    unnamed x1, local copies, waits for them, and re-layouts: 1.67 us -> 0.71 us
where the time goes in v3:
time: 34.8 us; the launch traced here: 34.7 us
  Pallas kernels  33.3 us (96%)
  local copies, waits for them, and re-layouts  0.71 us (2%)
  between operations  0.66 us (2%)
    pallas_call x1, Pallas kernels, local(): pl.pallas_call(body, out_shape=pltpu.VMEM((16, NPHI), F32), in_specs=[any...  33.3 us
    unnamed x1, local copies, waits for them, and re-layouts  0.71 us

profile of v3, /device:TPU:1, one launch (start us, length us, event | category | flops | bytes accessed | tf_op | source)
XLA Modules:
  0.0 34.7 jit_solution(17979908808009888527)
XLA Ops:
  0.7 33.3 %shard_map.64 = f32[16,4096]{1,0:T(8,128)S(1)} custom-call(f32[1,2,32,1024]{3,2,1,0:T(8,128)} %vis_hbm.1, s32[8,128]{1,0:T(8,128)} %bitcast.2, s32[1]{0:T(128)S(6)} %copy.9.band_hbm, bf16[1,1,2,1024,1024]{4,3,2,1,0:T(8,128)(2,1)} %beam_hbm.1, bf16[1,1024,1024]{2,1,0:T(8,128)(2,1)} %leg_hbm.1, s32[8,128]{1,0:T(8,128)} %bitcast.3), custom_call_target="tpu_custom_call" | custom-call | tf_op jit(solution)/shard_map/pallas_call | solution.py:293
  34.0 0.7 %copy.8 = f32[16,4096]{1,0:T(8,128)} copy(f32[16,4096]{1,0:T(8,128)S(1)} %shard_map.64) | data formatting | bytes 524288

commit v4 on v3

--- a/solution.py
+++ b/solution.py
@@ -40,6 +40,14 @@
 
 
 FAR_FIRST = sorted(range(1, 16), key=hops, reverse=True)
+
+
+def all_hops(d):
+    freq = (0, 1, 2, 1)[d // 64]
+    return hops(d // 16 % 4 * 4 + d // 2 % 4) + 4 * (d // 8 % 2) + freq * (1 - d // 8 % 2)
+
+
+ALL_FAR_FIRST = sorted(range(1, 256), key=all_hops, reverse=True)
 COLUMN = [q for q in range(1, 16) if q % 4 >= 2] + [q for q in range(1, 16) if q % 4 < 2]
 
 
@@ -71,9 +79,6 @@
     b_recv,
     c_send,
     c_recv,
-    d_send,
-    d_recv,
-    turned,
     load_sem,
     a_ssem,
     a_rsem,
@@ -83,8 +88,6 @@
     b_rsem,
     c_ssem,
     c_rsem,
-    d_ssem,
-    d_rsem,
 ):
     f = lax.axis_index("freq")
     s = lax.axis_index("shard")
@@ -95,6 +98,11 @@
 
     def plane(d):
         return f, shard_of((x + d // 4) % 4, zh, (y + d % 4) % 4, c)
+
+    def anyone(d):
+        return (f + d // 64) % 4, shard_of(
+            (x + d // 16 % 4) % 4, (zh + d // 8 % 2) % 2, (y + d // 2 % 4) % 4, (c + d % 2) % 2
+        )
 
     def column(df, e):
         return (f + df) % 4, shard_of(x, (zh + e // 2) % 2, y, (c + e % 2) % 2)
@@ -167,23 +175,8 @@
 
     loads[1].wait()
     stored = index[...]
-    lane = iota((8, 128), 1)
-    group = lane >> 4
-    pieces = []
-    for block in range(4):
-        for half in range(2):
-            joined = jnp.zeros((8, 128), I32)
-            for part in range(8):
-                px, py = half * 2 + part // 4, part % 4
-                source = py * 2 + block % 2
-                line = jnp.broadcast_to(stored[px * 2 + block // 2 : px * 2 + block // 2 + 1], (8, 128))
-                shift = ((part - source) * 16) % 128
-                if shift:
-                    line = pltpu.roll(line, shift, 1)
-                joined = jnp.where(group == part, line, joined)
-            pieces.append(joined)
     for piece in range(8):
-        wanted = jnp.broadcast_to(pieces[piece][0:1], (1024, 128))
+        wanted = jnp.broadcast_to(stored[piece : piece + 1], (1024, 128))
         onehot[:, piece * 128 : piece * 128 + 128] = jnp.where(
             iota((1024, 128), 0) == wanted, 1.0, 0.0
         ).astype(BF16)
@@ -193,17 +186,17 @@
             leg[...], onehot[:, block * 256 : block * 256 + 256], preferred_element_type=F32
         ).astype(BF16)
 
-    def sender_mode(r):
-        d, e = r >> 3, (r >> 1) & 3
-        return mode_of((x - (d >> 2)) & 3, (zh + (e >> 1)) & 1, (y - (d & 3)) & 3, (c + e) & 1)
+    def sender_mode(lane):
+        d = lane & 63
+        return mode_of((x - (d >> 4)) & 3, (zh + (d >> 3)) & 1, (y - (d >> 1)) & 3, (c + d) & 1)
 
     row, col = iota((128, 128), 0), iota((128, 128), 1)
-    fine = cosine((first + sender_mode(row)) * col + (row & 1) * (NPHI // 4), NPHI)
+    fine = cosine((first + sender_mode(row)) * col + (row >> 6) * (NPHI // 4), NPHI)
     fine_hi, fine_lo = split(fine * (1.0 / math.sqrt(128.0)))
     row, col = iota((32, 128), 0), iota((32, 128), 1)
     turns = (first + sender_mode(col)) * row
     coarse_cos = cosine(turns, 32)
-    coarse_sin = cosine(turns + 8 - 16 * (col & 1), 32)
+    coarse_sin = cosine(turns + 8 - 16 * (col >> 6), 32)
 
     loads[2].wait()
     weight8 = counts[...].astype(F32) * (0.125 / math.sqrt(NT))
@@ -235,44 +228,26 @@
     alm = alm + lax.dot_general(crossed, beam[1], over_b, preferred_element_type=F32)
     cycles = jnp.dot(alm.astype(BF16), chosen[...], preferred_element_type=F32)
 
-    for block in range(4):
-        c_send[block] = cycles[0:2, block * 256 : block * 256 + 256]
-    c_copies = {}
-    for q in COLUMN:
-        e = q % 4
-        block = ((zh + e // 2) % 2) * 2 + (c + e % 2) % 2
-        c_copies[q] = send(
-            c_send.at[block], c_recv.at[q], c_ssem.at[q], c_rsem.at[q], column(q // 4, e)
-        )
-    mine = c_send[zh * 2 + c]
-    sums = []
-    for e in range(4):
-        summed = mine
-        for df in range(4):
-            q = df * 4 + e
-            if q:
-                c_copies[q].wait_recv()
-            if df == 0:
-                summed = c_recv[q] if q else mine
-            else:
-                summed = summed + c_recv[q]
-        sums.append(summed)
-    gathered = jnp.concatenate(sums, axis=0)
-    d_send[0] = gathered[:, 0:128]
-    d_send[1] = gathered[:, 128:256]
-
-    d_copies = []
-    for d in FAR_FIRST:
-        half = ((x + d // 4) % 4) // 2
-        d_copies.append(send(d_send.at[half], d_recv.at[d], d_ssem.at[d], d_rsem.at[d], plane(d)))
-    d_recv[0] = d_send[x // 2]
-    for copy in d_copies:
-        copy.wait_recv()
-    turned[...] = d_recv[...].reshape(128, 128).T
-    place = (x % 2) * 4 + y
-    values = turned[pl.ds(pl.multiple_of(place * 16, 16), 16), :]
-    odd = (iota((16, 128), 1) & 1) == 1
-    swapped = jnp.where(odd, pltpu.roll(values, 1, 1), pltpu.roll(values, 127, 1))
+    real = jnp.concatenate([cycles[0:1, i * 128 : i * 128 + 128] for i in range(8)], axis=0)
+    imag = jnp.concatenate([cycles[1:2, i * 128 : i * 128 + 128] for i in range(8)], axis=0)
+    first_lanes = iota((8, 128), 1) < 16
+    for b in range(8):
+        left = pltpu.roll(real, (128 - 16 * b) % 128, 1) if b else real
+        right = pltpu.roll(imag, (144 - 16 * b) % 128, 1) if b != 1 else imag
+        c_send[b * 8 : b * 8 + 8] = jnp.where(first_lanes, left, right).reshape(8, 1, 128)
+
+    def row_of(shard):
+        return shard % 8 * 8 + shard // 8
+
+    for d in ALL_FAR_FIRST:
+        target = anyone(d)
+        send(c_send.at[row_of(target[1])], c_recv.at[d], c_ssem, c_rsem, target)
+    c_recv[0] = c_send[row_of(s)]
+    pltpu.make_async_copy(c_recv.at[1:256], c_recv.at[1:256], c_rsem).wait()
+    summed = c_recv[0:64] + c_recv[64:128] + c_recv[128:192] + c_recv[192:256]
+    summed = jnp.concatenate([summed.reshape(64, 128), jnp.zeros((64, 128), F32)], axis=0).T
+    values = summed[0:16] + pltpu.roll(summed[16:32], 64, 1)
+    swapped = pltpu.roll(values, 64, 1)
     moved = jnp.concatenate(
         [values * coarse_cos[a : a + 1] + swapped * coarse_sin[a : a + 1] for a in range(32)], axis=0
     )
@@ -283,8 +258,9 @@
     for a in range(32):
         out_ref[:, a * 128 : a * 128 + 128] = image[a * 16 : a * 16 + 16]
 
-    for copy in step_copies + a_copies + b_copies + list(c_copies.values()) + d_copies:
+    for copy in step_copies + a_copies + b_copies:
         copy.wait_send()
+    pltpu.make_async_copy(c_recv.at[1:256], c_recv.at[1:256], c_ssem).wait()
 
 
 def local(vis, counts, band_start, beam, legendre, cycle_index):
@@ -317,11 +293,8 @@
             pltpu.VMEM((16, 1, 128), F32),
             pltpu.VMEM((4, 2, 1024), F32),
             pltpu.VMEM((4, 2, 1024), F32),
-            pltpu.VMEM((4, 2, 256), F32),
-            pltpu.VMEM((16, 2, 256), F32),
-            pltpu.VMEM((2, 8, 128), F32),
-            pltpu.VMEM((16, 8, 128), F32),
-            pltpu.VMEM((128, 128), F32),
+            pltpu.VMEM((64, 1, 128), F32),
+            pltpu.VMEM((256, 1, 128), F32),
             dma((7,)),
             dma((16,)),
             dma((16,)),
@@ -329,10 +302,8 @@
             dma((16,)),
             dma((4,)),
             dma((4,)),
-            dma((16,)),
-            dma((16,)),
-            dma((16,)),
-            dma((16,)),
+            dma,
+            dma,
         ],
         compiler_params=pltpu.CompilerParams(
             collective_id=0, has_side_effects=True, vmem_limit_bytes=56 * 1024 * 1024

time: 34.8 us -> 32.9 us (0.945)
  Pallas kernels: 33.3 us -> 31.5 us
    pallas_call x1, Pallas kernels: 33.3 us -> 31.5 us  [local(): pl.pallas_call(body, out_shape=pltpu.VMEM((16, NPHI), F32), in_specs=[any...]
where the time goes in v4:
time: 32.9 us
  Pallas kernels  31.5 us (96%)
  local copies, waits for them, and re-layouts  0.71 us (2%)
  between operations  0.66 us (2%)
    pallas_call x1, Pallas kernels, local(): pl.pallas_call(body, out_shape=pltpu.VMEM((16, NPHI), F32), in_specs=[any...  31.5 us
    unnamed x1, local copies, waits for them, and re-layouts  0.71 us

profile of v4, /device:TPU:1, one launch (start us, length us, event | category | flops | bytes accessed | tf_op | source)
XLA Modules:
  0.0 32.9 jit_solution(15452737159797254761)
XLA Ops:
  0.7 31.5 %shard_map.64 = f32[16,4096]{1,0:T(8,128)S(1)} custom-call(f32[1,2,32,1024]{3,2,1,0:T(8,128)} %vis_hbm.1, s32[8,128]{1,0:T(8,128)} %bitcast.2, s32[1]{0:T(128)S(6)} %copy.9.band_hbm, bf16[1,1,2,1024,1024]{4,3,2,1,0:T(8,128)(2,1)} %beam_hbm.1, bf16[1,1024,1024]{2,1,0:T(8,128)(2,1)} %leg_hbm.1, s32[8,128]{1,0:T(8,128)} %bitcast.3), custom_call_target="tpu_custom_call" | custom-call | tf_op jit(solution)/shard_map/pallas_call | solution.py:269
  32.1 0.7 %copy.8 = f32[16,4096]{1,0:T(8,128)} copy(f32[16,4096]{1,0:T(8,128)S(1)} %shard_map.64) | data formatting | bytes 524288

commit v5 on v4

--- a/solution.py
+++ b/solution.py
@@ -71,6 +71,7 @@
     index,
     onehot,
     chosen,
+    across,
     a_send,
     a_recv,
     step_send,
@@ -186,6 +187,12 @@
             leg[...], onehot[:, block * 256 : block * 256 + 256], preferred_element_type=F32
         ).astype(BF16)
 
+    loads[4].wait()
+    for part in range(2):
+        for block in range(4):
+            lanes = slice(block * 256, block * 256 + 256)
+            across[part * 1024 + block * 256 : part * 1024 + block * 256 + 256, :] = beam[part, :, lanes].T
+
     def sender_mode(lane):
         d = lane & 63
         return mode_of((x - (d >> 4)) & 3, (zh + (d >> 3)) & 1, (y - (d >> 1)) & 3, (c + d) & 1)
@@ -203,7 +210,7 @@
     weight = jnp.concatenate([weight8[i : i + 1] for i in range(8)], axis=1)
 
     total = jnp.concatenate([partial[0:8, 0:512], partial[0:8, 512:1024]], axis=0)
-    for d, step_copy, copy in reversed(list(zip(FAR_FIRST, step_copies, a_copies))):
+    for d, step_copy, copy in zip(FAR_FIRST, step_copies, a_copies):
         step_copy.wait_recv()
         copy.wait_recv()
         step = jnp.concatenate([step_recv[d]] * 4, axis=1)
@@ -222,10 +229,8 @@
     zeros = jnp.zeros((14, 1024), F32)
     direct = jnp.concatenate([modes, zeros], axis=0).astype(BF16)
     crossed = jnp.concatenate([modes[1:2], -modes[0:1], zeros], axis=0).astype(BF16)
-    loads[4].wait()
-    over_b = (((1,), (1,)), ((), ()))
-    alm = lax.dot_general(direct, beam[0], over_b, preferred_element_type=F32)
-    alm = alm + lax.dot_general(crossed, beam[1], over_b, preferred_element_type=F32)
+    both = jnp.concatenate([direct, crossed], axis=1)
+    alm = jnp.dot(both, across[...], preferred_element_type=F32)
     cycles = jnp.dot(alm.astype(BF16), chosen[...], preferred_element_type=F32)
 
     real = jnp.concatenate([cycles[0:1, i * 128 : i * 128 + 128] for i in range(8)], axis=0)
@@ -241,11 +246,11 @@
 
     for d in ALL_FAR_FIRST:
         target = anyone(d)
-        send(c_send.at[row_of(target[1])], c_recv.at[d], c_ssem, c_rsem, target)
-    c_recv[0] = c_send[row_of(s)]
+        send(c_send.at[row_of(target[1])], c_recv.at[d : d + 1], c_ssem, c_rsem, target)
+    c_recv[0:1] = c_send[row_of(s)]
     pltpu.make_async_copy(c_recv.at[1:256], c_recv.at[1:256], c_rsem).wait()
     summed = c_recv[0:64] + c_recv[64:128] + c_recv[128:192] + c_recv[192:256]
-    summed = jnp.concatenate([summed.reshape(64, 128), jnp.zeros((64, 128), F32)], axis=0).T
+    summed = jnp.concatenate([summed, jnp.zeros((64, 128), F32)], axis=0).T
     values = summed[0:16] + pltpu.roll(summed[16:32], 64, 1)
     swapped = pltpu.roll(values, 64, 1)
     moved = jnp.concatenate(
@@ -287,6 +292,7 @@
             pltpu.VMEM((8, 128), I32),
             pltpu.VMEM((1024, 1024), BF16),
             pltpu.VMEM((1024, 1024), BF16),
+            pltpu.VMEM((2048, 1024), BF16),
             pltpu.VMEM((16, 16, 512), jnp.int16),
             pltpu.VMEM((16, 16, 512), jnp.int16),
             pltpu.VMEM((16, 1, 128), F32),
@@ -294,7 +300,7 @@
             pltpu.VMEM((4, 2, 1024), F32),
             pltpu.VMEM((4, 2, 1024), F32),
             pltpu.VMEM((64, 1, 128), F32),
-            pltpu.VMEM((256, 1, 128), F32),
+            pltpu.VMEM((256, 128), F32),
             dma((7,)),
             dma((16,)),
             dma((16,)),

time: 32.9 us -> 32.3 us (0.982)
  Pallas kernels: 31.5 us -> 30.9 us
    pallas_call x1, Pallas kernels: 31.5 us -> 30.9 us  [local(): pl.pallas_call(body, out_shape=pltpu.VMEM((16, NPHI), F32), in_specs=[any...]
where the time goes in v5:
time: 32.3 us
  Pallas kernels  30.9 us (96%)
  local copies, waits for them, and re-layouts  0.71 us (2%)
  between operations  0.66 us (2%)
    pallas_call x1, Pallas kernels, local(): pl.pallas_call(body, out_shape=pltpu.VMEM((16, NPHI), F32), in_specs=[any...  30.9 us
    unnamed x1, local copies, waits for them, and re-layouts  0.71 us

profile of v5, /device:TPU:1, one launch (start us, length us, event | category | flops | bytes accessed | tf_op | source)
XLA Modules:
  0.0 32.3 jit_solution(14543367563573165508)
XLA Ops:
  0.7 30.9 %shard_map.64 = f32[16,4096]{1,0:T(8,128)S(1)} custom-call(f32[1,2,32,1024]{3,2,1,0:T(8,128)} %vis_hbm.1, s32[8,128]{1,0:T(8,128)} %bitcast.2, s32[1]{0:T(128)S(6)} %copy.9.band_hbm, bf16[1,1,2,1024,1024]{4,3,2,1,0:T(8,128)(2,1)} %beam_hbm.1, bf16[1,1024,1024]{2,1,0:T(8,128)(2,1)} %leg_hbm.1, s32[8,128]{1,0:T(8,128)} %bitcast.3), custom_call_target="tpu_custom_call" | custom-call | tf_op jit(solution)/shard_map/pallas_call | solution.py:274
  31.6 0.7 %copy.8 = f32[16,4096]{1,0:T(8,128)} copy(f32[16,4096]{1,0:T(8,128)S(1)} %shard_map.64) | data formatting | bytes 524288

commit v6 on v5

--- a/solution.py
+++ b/solution.py
@@ -63,6 +63,10 @@
     leg_hbm,
     index_hbm,
     out_ref,
+    cos_ref,
+    sin_ref,
+    high_ref,
+    low_ref,
     vis,
     counts,
     band,
@@ -205,6 +209,11 @@
     coarse_cos = cosine(turns, 32)
     coarse_sin = cosine(turns + 8 - 16 * (col >> 6), 32)
 
+    cos_ref[...] = coarse_cos
+    sin_ref[...] = coarse_sin
+    high_ref[...] = fine_hi
+    low_ref[...] = fine_lo
+
     loads[2].wait()
     weight8 = counts[...].astype(F32) * (0.125 / math.sqrt(NT))
     weight = jnp.concatenate([weight8[i : i + 1] for i in range(8)], axis=1)
@@ -252,28 +261,53 @@
     summed = c_recv[0:64] + c_recv[64:128] + c_recv[128:192] + c_recv[192:256]
     summed = jnp.concatenate([summed, jnp.zeros((64, 128), F32)], axis=0).T
     values = summed[0:16] + pltpu.roll(summed[16:32], 64, 1)
-    swapped = pltpu.roll(values, 64, 1)
-    moved = jnp.concatenate(
-        [values * coarse_cos[a : a + 1] + swapped * coarse_sin[a : a + 1] for a in range(32)], axis=0
-    )
-    moved_hi, moved_lo = split(moved)
-    image = jnp.dot(moved_hi, fine_hi, preferred_element_type=F32)
-    image = image + jnp.dot(moved_lo, fine_hi, preferred_element_type=F32)
-    image = image + jnp.dot(moved_hi, fine_lo, preferred_element_type=F32)
-    for a in range(32):
-        out_ref[:, a * 128 : a * 128 + 128] = image[a * 16 : a * 16 + 16]
-
+    out_ref[...] = values
     for copy in step_copies + a_copies + b_copies:
         copy.wait_send()
     pltpu.make_async_copy(c_recv.at[1:256], c_recv.at[1:256], c_ssem).wait()
 
 
+def paint(values_ref, cos_ref, sin_ref, high_ref, low_ref, out_hbm, pieces, sem):
+    values = values_ref[...]
+    swapped = pltpu.roll(values, 64, 1)
+    fine_hi, fine_lo = high_ref[...], low_ref[...]
+    copies = []
+    for piece in range(4):
+        moved = jnp.concatenate(
+            [
+                values * cos_ref[a : a + 1] + swapped * sin_ref[a : a + 1]
+                for a in range(piece * 8, piece * 8 + 8)
+            ],
+            axis=0,
+        )
+        moved_hi, moved_lo = split(moved)
+        image = jnp.dot(moved_hi, fine_hi, preferred_element_type=F32)
+        image = image + jnp.dot(moved_lo, fine_hi, preferred_element_type=F32)
+        image = image + jnp.dot(moved_hi, fine_lo, preferred_element_type=F32)
+        for a in range(8):
+            pieces[piece, :, a * 128 : a * 128 + 128] = image[a * 16 : a * 16 + 16]
+        copy = pltpu.make_async_copy(
+            pieces.at[piece], out_hbm.at[:, piece * 1024 : piece * 1024 + 1024], sem.at[piece]
+        )
+        copy.start()
+        copies.append(copy)
+    for copy in copies:
+        copy.wait()
+
+
 def local(vis, counts, band_start, beam, legendre, cycle_index):
     anywhere = pl.BlockSpec(memory_space=pl.ANY)
     dma = pltpu.SemaphoreType.DMA
-    return pl.pallas_call(
+    vmem = pl.BlockSpec(memory_space=pltpu.VMEM)
+    tables = pl.pallas_call(
         body,
-        out_shape=pltpu.VMEM((16, NPHI), F32),
+        out_shape=(
+            pltpu.VMEM((16, 128), F32),
+            pltpu.VMEM((32, 128), F32),
+            pltpu.VMEM((32, 128), F32),
+            pltpu.VMEM((128, 128), BF16),
+            pltpu.VMEM((128, 128), BF16),
+        ),
         in_specs=[
             anywhere,
             anywhere,
@@ -282,7 +316,7 @@
             anywhere,
             anywhere,
         ],
-        out_specs=pl.BlockSpec(memory_space=pltpu.VMEM),
+        out_specs=[vmem] * 5,
         scratch_shapes=[
             pltpu.VMEM((2, 32, 1024), F32),
             pltpu.VMEM((8, 128), I32),
@@ -322,6 +356,15 @@
         legendre,
         cycle_index.reshape(8, 128),
     )
+    tables = [pltpu.with_memory_space_constraint(table, pltpu.VMEM) for table in tables]
+    return pl.pallas_call(
+        paint,
+        out_shape=jax.ShapeDtypeStruct((16, NPHI), F32),
+        in_specs=[vmem] * 5,
+        out_specs=anywhere,
+        scratch_shapes=[pltpu.VMEM((4, 16, 1024), F32), dma((4,))],
+    )(*tables)
+
 
 def solution(mesh):
     return jax.shard_map(

time: 32.3 us -> 32.2 us (level)
  local copies, waits for them, and re-layouts: 0.71 us -> 0 us
  Pallas kernels: 30.9 us -> 31.5 us
    unnamed x1 -> x0, local copies, waits for them, and re-layouts: 0.71 us -> none
    pallas_call x1 -> x2, Pallas kernels: 30.9 us -> 31.5 us  [the longest x1 30.5 us: local(): pl.pallas_call(body, out_shape=(pltpu.VMEM((16, 128), F32), pltpu.VMEM((3...]
where the time goes in v6:
time: 32.2 us; the launch traced here: 32.1 us
  Pallas kernels  31.5 us (98%)
  between operations  0.66 us (2%)
    pallas_call x1, Pallas kernels, local(): pl.pallas_call(body, out_shape=(pltpu.VMEM((16, 128), F32), pltpu.VMEM((3...  30.5 us
    pallas_call x1, Pallas kernels, local(): pl.pallas_call(paint, out_shape=jax.ShapeDtypeStruct((16, NPHI), F32), in...  1.02 us

profile of v6, /device:TPU:1, one launch (start us, length us, event | category | flops | bytes accessed | tf_op | source)
XLA Modules:
  0.0 32.1 jit_solution(13430920355846314987)
XLA Ops:
  0.7 30.5 %shard_map.64 = (f32[16,128]{1,0:T(8,128)S(1)}, f32[32,128]{1,0:T(8,128)S(1)}, f32[32,128]{1,0:T(8,128)S(1)}, bf16[128,128]{1,0:T(8,128)(2,1)S(1)}, bf16[128,128]{1,0:T(8,128)(2,1)S(1)}) custom-call(f32[1,2,32,1024]{3,2,1,0:T(8,128)} %vis_hbm.1, s32[8,128]{1,0:T(8,128)} %bitcast.2, s32[1]{0:T(128)S(6)} %copy.7.band_hbm, ...), custom_call_target="tpu_custom_call" | custom-call | tf_op jit(solution)/shard_map/pallas_call | solution.py:302
  31.1 1.0 %shard_map.65 = f32[16,4096]{1,0:T(8,128)} custom-call(f32[16,128]{1,0:T(8,128)S(1)} %get-tuple-element.10.values_ref, f32[32,128]{1,0:T(8,128)S(1)} %get-tuple-element.11.cos_ref, f32[32,128]{1,0:T(8,128)S(1)} %get-tuple-element.12.sin_ref, bf16[128,128]{1,0:T(8,128)(2,1)S(1)} %get-tuple-element.13.high_ref, bf16[128,128]{1,0:T(8,128)(2,1)S(1)} %get-tuple-element.14.low_ref), custom_call_target="tpu_custom_call" | custom-call | tf_op jit(solution)/shard_map/pallas_call | solution.py:360
